TPU v7x, 32 devices: a whole 2x2x4 slice. The times are simulated.
32 devices in a mesh: row: 4 (over x, core), col: 8 (over z, y).
Axes of the slice: x: 2, y: 2, z: 4, core: 2. Of those that a mesh axis runs over, the one named last changes fastest.
Arguments:
- src_coords: int32 [3, 65536], P(None, 'row'), may hold values from 0 to 51
- tgt_coords: int32 [3, 65536], P(None, 'col'), may hold values from 0 to 51
- src_mass: int32 [65536], P('row'), may hold values from 1 to 298
- tgt_mass: int32 [65536], P('col'), may hold values from 1 to 298
- tgt_start: float32 [65536], P('col'), may hold values from -10 to 170
- kept_src: int32 [4, 8, 64], P('row', 'col'), may hold values from 0 to 127, as said below
- kept_tgt: int32 [4, 8, 64], P('row', 'col'), may hold values from 0 to 63, as said below
- kept_count: int32 [4, 8], P('row', 'col'), may hold values from 1 to 64, as said below
Outputs:
- src_potential: float32 [65536], P('row')
- tgt_potential: float32 [65536], P('col')
Inputs may be any that keep to these rules, and one draw needn't show every extreme that they name: `kept_src`: every source tile lies in a live pair of some device of its row block. Slots at or past a device's count hold pairs that are not live. `kept_tgt`: every target tile lies in a live pair of some device of its column block. `kept_count`: some device has exactly 64 live slots in every draw.
All inputs are finite; a program needn't handle non-finite values.
Results may differ from a plain program's by a relative error of at most 0.0001.
Values sent between devices are 32-bit elements; how exact they have to be, the bound alone decides.
A program may use at most 64 MiB of HBM per device.

v0:
```python
import functools
import math

import jax
import jax.numpy as jnp
from jax import lax
from jax.experimental import pallas as pl
from jax.experimental.pallas import tpu as pltpu
from jax.sharding import PartitionSpec as P

ITERS = 3
LANES = 128
NEG = -1e30
CENTRE = 26.0
UNROLL = 8
SLOT_UNROLL = 32
MESH = pl.DeviceIdType.MESH

COST = 0.05
EXP2 = COST * math.log2(math.e)


def order_slots(ids, others, live, tiles):
    slots = ids.shape[1]
    lane = lax.broadcasted_iota(jnp.int32, (slots, slots), 1)
    sub = lax.broadcasted_iota(jnp.int32, (slots, slots), 0)

    def column(row):
        spread = jnp.broadcast_to(row, (slots, slots))
        return jnp.sum(jnp.where(lane == sub, spread, 0), axis=1, keepdims=True)

    key = jnp.where(live, ids, tiles) * slots + lane[0:1, :]
    mine = jnp.where(live, ids, tiles)
    key_col, mine_col = column(key), column(mine)
    before = (key < key_col).astype(jnp.int32)
    rank_col = jnp.sum(before, axis=1, keepdims=True)
    after = (key_col < key).astype(jnp.int32)
    rank = jnp.sum(after, axis=0, keepdims=True)
    hit = rank_col == lane
    sorted_ids = jnp.sum(jnp.where(hit, column(ids), 0), axis=0, keepdims=True)
    sorted_others = jnp.sum(jnp.where(hit, column(others), 0), axis=0, keepdims=True)
    earlier = (mine_col == mine) & (sub < lane)
    place = jnp.sum(earlier.astype(jnp.int32), axis=0, keepdims=True)
    place = jnp.where(live, place, -1)
    place = jnp.sum(
        jnp.where(rank == sub, jnp.broadcast_to(place, (slots, slots)), 0), axis=1, keepdims=True
    )
    tile = lax.broadcasted_iota(jnp.int32, (slots, LANES), 1)
    upto = jnp.sum((mine_col <= tile).astype(jnp.int32), axis=0, keepdims=True)
    held = jnp.sum((mine_col == tile).astype(jnp.int32), axis=0, keepdims=True)
    last = jnp.where(held > 0, upto - 1, slots)
    return sorted_ids, sorted_others, last, jnp.broadcast_to(place, (slots, LANES))


def kernel(
    n_row, n_col,
    count, kept_src, kept_tgt, src_xyz_in, tgt_xyz_in, src_mass_in, tgt_mass_in, start_in,
    src_out, tgt_out,
    src_ids, tgt_ids, src_xyz, tgt_xyz, src_mass, tgt_mass, start, load_sems,
    idx_rows, idx, idx_sem, place_s, place_t,
    a_src, b_src, a_tgt, b_tgt, sq_src, sq_tgt, log_src, log_tgt,
    hat_src, hat_tgt, peak, total, runs, send_src, got_src, got_tgt,
    mass_src, mass_tgt, mass_sems, src_sems, tgt_sems,
):
    row, col = lax.axis_index("row"), lax.axis_index("col")
    slots = place_s.shape[0]
    sublane = lax.broadcasted_iota(jnp.int32, (8, LANES), 0)

    loads = [
        pltpu.make_async_copy(src, dst, load_sems.at[k])
        for k, (src, dst) in enumerate((
            (kept_src, src_ids), (kept_tgt, tgt_ids), (src_mass_in, src_mass),
            (tgt_mass_in, tgt_mass), (src_xyz_in, src_xyz), (tgt_xyz_in, tgt_xyz),
            (start_in, start),
        ))
    ]
    for load in loads:
        load.start()

    barrier = pltpu.get_barrier_semaphore()
    for axis, me, n in (("row", row, n_row), ("col", col, n_col)):
        for off in range(1, n):
            pl.semaphore_signal(
                barrier, inc=1, device_id={axis: lax.rem(me + off, n)}, device_id_type=MESH
            )

    for load in loads[:2]:
        load.wait()
    live = lax.broadcasted_iota(jnp.int32, (1, slots), 1) < count[0, 0]
    idx_rows[...] = jnp.zeros_like(idx_rows)
    for k, (ids, others, place, tiles) in enumerate((
        (src_ids, tgt_ids, place_s, a_src.shape[0]), (tgt_ids, src_ids, place_t, a_tgt.shape[0]),
    )):
        mine, theirs, last, place[...] = order_slots(ids[...], others[...], live, tiles)
        idx_rows[3 * k : 3 * k + 1, 0:slots] = mine
        idx_rows[3 * k + 1 : 3 * k + 2, 0:slots] = theirs
        idx_rows[3 * k + 2 : 3 * k + 3, :] = last
    to_scalars = pltpu.make_async_copy(idx_rows, idx, idx_sem)
    to_scalars.start()
    for load in loads[2:4]:
        load.wait()
    for mass, held, me in ((src_mass, mass_src, row), (tgt_mass, mass_tgt, col)):
        lane_sum = jnp.sum(
            mass[...].reshape(-1, LANES), axis=0, keepdims=True
        )
        held[me] = jnp.broadcast_to(lane_sum.astype(jnp.float32), (8, LANES))

    pl.semaphore_wait(barrier, n_row + n_col - 2)

    mass_copies = []
    for axis, held, me, n, base in (
        ("row", mass_src, row, n_row, 0), ("col", mass_tgt, col, n_col, n_row - 1),
    ):
        for off in range(1, n):
            copy = pltpu.make_async_remote_copy(
                src_ref=held.at[me], dst_ref=held.at[me],
                send_sem=mass_sems.at[0, base + off - 1], recv_sem=mass_sems.at[1, base + off - 1],
                device_id={axis: lax.rem(me + off, n)}, device_id_type=MESH,
            )
            copy.start()
            mass_copies.append(copy)

    def set_up(xyz, a_ref, b_ref, sq_ref):
        def step(block, carry):
            for u in range(UNROLL):
                t = block * UNROLL + u
                at = pl.ds(pl.multiple_of(t * LANES, LANES), LANES)
                x, y, z = (xyz[d : d + 1, at].astype(jnp.float32) - CENTRE for d in range(3))
                sq_ref[pl.ds(t, 1), :] = x * x + y * y + z * z
                rows = jnp.where(
                    sublane == 0, x, jnp.where(sublane == 1, y, jnp.where(sublane == 2, z, 0.0))
                )
                a_ref[t] = rows
                b_ref[t] = jnp.where(sublane < 3, 2.0 * rows, jnp.where(sublane < 6, 1.0, 0.0))
            return carry

        lax.fori_loop(0, a_ref.shape[0] // UNROLL, step, 0)

    for load in loads[4:]:
        load.wait()
    set_up(src_xyz, a_src, b_src, sq_src)
    set_up(tgt_xyz, a_tgt, b_tgt, sq_tgt)
    hat_tgt[0] = start[...] * (1.0 / COST) - sq_tgt[...]
    runs[pl.ds(slots, 8), :] = jnp.full((8, LANES), NEG, jnp.float32)
    to_scalars.wait()

    def partials(load_hat, a_ref, b_ref, in_row, out_row, place):
        def step(block, carry):
            for u in range(SLOT_UNROLL):
                p = block * SLOT_UNROLL + u
                i_in, i_out = idx[in_row, p], idx[out_row, p]
                hat = jnp.broadcast_to(load_hat(i_in), (8, LANES))
                high = hat.astype(jnp.bfloat16).astype(jnp.float32)
                rest = hat - high
                mid = rest.astype(jnp.bfloat16).astype(jnp.float32)
                a = jnp.where(
                    sublane == 3, high,
                    jnp.where(sublane == 4, mid, jnp.where(sublane == 5, rest - mid, a_ref[i_in])),
                ).astype(jnp.bfloat16)
                scores = lax.dot_general(
                    a, b_ref[i_out].astype(jnp.bfloat16), (((0,), (0,)), ((), ())),
                    preferred_element_type=jnp.float32,
                )
                top = jnp.max(scores, axis=0, keepdims=True)
                peak[pl.ds(p, 1), :] = top
                total[pl.ds(p, 1), :] = jnp.sum(
                    jnp.exp2((scores - top) * EXP2), axis=0, keepdims=True
                )
            return carry

        lax.fori_loop(0, slots // SLOT_UNROLL, step, 0)
        where_in = place[...]
        lse = jnp.where(where_in >= 0, peak[...] * COST + jnp.log(total[...]), NEG)
        reach = 1
        while reach < slots:
            before = pltpu.roll(lse, reach, axis=0)
            both = jnp.maximum(lse, before) + jnp.log(1.0 + jnp.exp(-jnp.abs(lse - before)))
            lse = jnp.where(where_in >= reach, both, lse)
            reach *= 2
        runs[pl.ds(0, slots), :] = lse

    def send(axis, me, n, off, src, dst, sems):
        copy = pltpu.make_async_remote_copy(
            src_ref=src, dst_ref=dst, send_sem=sems.at[0, off - 1], recv_sem=sems.at[1, off - 1],
            device_id={axis: lax.rem(me + off, n)}, device_id_type=MESH,
        )
        copy.start()
        return copy

    def merged(parts):
        top = functools.reduce(jnp.maximum, parts)
        return top + jnp.log(functools.reduce(jnp.add, [jnp.exp(part - top) for part in parts]))

    def merge_src(it):
        tp = send_src.shape[1]
        first = []
        for off in range(n_col):
            peer = lax.rem(col + 1 + off, n_col)
            for u in range(tp):
                send_src[peer, u : u + 1, :] = runs[pl.ds(idx[2, peer * tp + u], 1), :]
            if off < n_col - 1:
                first.append(send(
                    "col", col, n_col, off + 1,
                    send_src.at[peer], got_src.at[it, col], src_sems.at[it, 0],
                ))
        for copy in first:
            copy.wait_recv()
        parts = [send_src[col]] + [
            got_src[it, lax.rem(col + off, n_col)] for off in range(1, n_col)
        ]
        hat_src[it, col] = (log_src[...] - merged(parts)) * (1.0 / COST)
        mine = hat_src.at[it, col]
        second = [
            send("col", col, n_col, off, mine, mine, src_sems.at[it, 1])
            for off in range(1, n_col)
        ]
        for copy in second:
            copy.wait_recv()
        for copy in first + second:
            copy.wait_send()

    def merge_tgt(it):
        tiles = got_tgt.shape[2]

        def pick(block, carry):
            for u in range(UNROLL * 2):
                t = block * (UNROLL * 2) + u
                got_tgt[it, row, pl.ds(t, 1), :] = runs[pl.ds(idx[5, t], 1), :]
            return carry

        lax.fori_loop(0, tiles // (UNROLL * 2), pick, 0)
        mine = got_tgt.at[it, row]
        copies = [
            send("row", row, n_row, off, mine, mine, tgt_sems.at[it]) for off in range(1, n_row)
        ]
        for copy in copies:
            copy.wait()
        parts = [got_tgt[it, r] for r in range(n_row)]
        hat_tgt[it + 1] = (log_tgt[...] - merged(parts)) * (1.0 / COST)

    def iterate(it, carry):
        partials(lambda t: hat_tgt[it, pl.ds(t, 1), :], a_tgt, b_src, 1, 0, place_s)
        merge_src(it)
        tp = hat_src.shape[2]
        partials(
            lambda t: hat_src[it, t // tp, pl.ds(t % tp, 1), :], a_src, b_tgt, 4, 3, place_t
        )
        merge_tgt(it)
        return carry

    for copy in mass_copies:
        copy.wait()
    src_all = jnp.sum(jnp.sum(mass_src[...], axis=0)[0:1, :], axis=1, keepdims=True)
    tgt_all = jnp.sum(jnp.sum(mass_tgt[...], axis=0)[0:1, :], axis=1, keepdims=True)
    log_src[...] = jnp.log(src_mass[col].astype(jnp.float32)) - jnp.log(src_all)
    log_tgt[...] = jnp.log(tgt_mass[...].astype(jnp.float32)) - jnp.log(tgt_all)
    lax.fori_loop(0, ITERS, iterate, 0)
    src_hat = hat_src[ITERS - 1].reshape(src_out.shape)
    src_out[...] = (src_hat + sq_src[...]) * COST
    tgt_out[...] = (hat_tgt[ITERS] + sq_tgt[...]) * COST


def on_device(
    n_row, n_col,
    src_coords, tgt_coords, src_mass, tgt_mass, tgt_start, kept_src, kept_tgt, kept_count,
):
    slots = kept_src.shape[-1]
    src_tiles, tgt_tiles = src_coords.shape[1] // LANES, tgt_coords.shape[1] // LANES
    src_split = (n_col, src_tiles // n_col, LANES)
    src_block, tgt_block = (src_tiles, LANES), (tgt_tiles, LANES)
    f32, i32 = jnp.float32, jnp.int32
    vmem = pl.BlockSpec(memory_space=pltpu.VMEM)
    src_out, tgt_out = pl.pallas_call(
        functools.partial(kernel, n_row, n_col),
        out_shape=(
            jax.ShapeDtypeStruct(src_block, f32),
            jax.ShapeDtypeStruct(tgt_block, f32),
        ),
        in_specs=[pl.BlockSpec(memory_space=pltpu.SMEM)] + [pl.BlockSpec(memory_space=pl.ANY)] * 7,
        out_specs=(vmem, vmem),
        scratch_shapes=[
            pltpu.VMEM((1, slots), i32),
            pltpu.VMEM((1, slots), i32),
            pltpu.VMEM(src_coords.shape, i32),
            pltpu.VMEM(tgt_coords.shape, i32),
            pltpu.VMEM(src_split, i32),
            pltpu.VMEM(tgt_block, i32),
            pltpu.VMEM(tgt_block, f32),
            pltpu.SemaphoreType.DMA((7,)),
            pltpu.VMEM((8, LANES), i32),
            pltpu.SMEM((8, LANES), i32),
            pltpu.SemaphoreType.DMA,
            pltpu.VMEM((slots, LANES), i32),
            pltpu.VMEM((slots, LANES), i32),
            pltpu.VMEM((src_tiles, 8, LANES), f32),
            pltpu.VMEM((src_tiles, 8, LANES), f32),
            pltpu.VMEM((tgt_tiles, 8, LANES), f32),
            pltpu.VMEM((tgt_tiles, 8, LANES), f32),
            pltpu.VMEM(src_block, f32),
            pltpu.VMEM(tgt_block, f32),
            pltpu.VMEM(src_split[1:], f32),
            pltpu.VMEM(tgt_block, f32),
            pltpu.VMEM((ITERS,) + src_split, f32),
            pltpu.VMEM((ITERS + 1,) + tgt_block, f32),
            pltpu.VMEM((slots, LANES), f32),
            pltpu.VMEM((slots, LANES), f32),
            pltpu.VMEM((slots + 8, LANES), f32),
            pltpu.VMEM(src_split, f32),
            pltpu.VMEM((ITERS,) + src_split, f32),
            pltpu.VMEM((ITERS, n_row) + tgt_block, f32),
            pltpu.VMEM((n_row, 8, LANES), f32),
            pltpu.VMEM((n_col, 8, LANES), f32),
            pltpu.SemaphoreType.DMA((2, n_row + n_col - 2)),
            pltpu.SemaphoreType.DMA((ITERS, 2, 2, n_col - 1)),
            pltpu.SemaphoreType.DMA((ITERS, 2, n_row - 1)),
        ],
        compiler_params=pltpu.CompilerParams(
            collective_id=0, has_side_effects=True, vmem_limit_bytes=48 * 1024 * 1024
        ),
        name="sinkhorn",
    )(
        kept_count, kept_src.reshape(1, slots), kept_tgt.reshape(1, slots),
        src_coords, tgt_coords,
        src_mass.reshape(src_split), tgt_mass.reshape(tgt_block), tgt_start.reshape(tgt_block),
    )
    return src_out.reshape(-1), tgt_out.reshape(-1)


def solution(mesh):
    placed = (
        P(None, "row"), P(None, "col"), P("row"), P("col"), P("col"),
        P("row", "col", None), P("row", "col", None), P("row", "col"),
    )
    return jax.shard_map(
        functools.partial(on_device, mesh.shape["row"], mesh.shape["col"]),
        mesh=mesh, in_specs=placed, out_specs=(P("row"), P("col")), check_vma=False,
    )
```

profile of v0, /device:TPU:0, one launch (start us, length us, event | category | flops | bytes accessed | tf_op | source)
XLA Modules:
  0.0 62.5 jit_solution(1532433695764219821)
XLA Ops:
  1.3 0.0 copy-start.5
  1.3 0.0 copy-start.6
  1.3 0.6 %copy-done.5 = s32[1,1,64]{2,1,0:T(1,128)S(1)} copy-done((s32[1,1,64]{2,1,0:T(1,128)S(1)}, s32[1,1,64]{2,1,0:T(1,128)}, u32[]{:S(2)}) %copy-start.5) | copy-done | bytes 280
  1.9 0.0 copy-done.6
  2.0 0.0 copy-start
  2.0 0.9 %copy-done = s32[3,16384]{1,0:T(4,128)S(1)} copy-done((s32[3,16384]{1,0:T(4,128)S(1)}, s32[3,16384]{1,0:T(4,128)}, u32[]{:S(2)}) %copy-start) | copy-done | bytes 196632
  2.9 0.0 copy-start.1
  2.9 0.9 %copy-done.1 = s32[3,8192]{1,0:T(4,128)S(1)} copy-done((s32[3,8192]{1,0:T(4,128)S(1)}, s32[3,8192]{1,0:T(4,128)}, u32[]{:S(2)}) %copy-start.1) | copy-done | bytes 98328
  3.8 0.0 copy-start.2
  3.8 0.8 %copy-done.2 = s32[16384]{0:T(1024)S(1)} copy-done((s32[16384]{0:T(1024)S(1)}, s32[16384]{0:T(1024)}, u32[]{:S(2)}) %copy-start.2) | copy-done | bytes 65560
  4.6 0.0 copy-start.3
  4.6 0.8 %copy-done.3 = s32[8192]{0:T(1024)S(1)} copy-done((s32[8192]{0:T(1024)S(1)}, s32[8192]{0:T(1024)}, u32[]{:S(2)}) %copy-start.3) | copy-done | bytes 32792
  5.4 0.0 copy-start.4
  5.4 0.8 %copy-done.4 = f32[8192]{0:T(1024)S(1)} copy-done((f32[8192]{0:T(1024)S(1)}, f32[8192]{0:T(1024)}, u32[]{:S(2)}) %copy-start.4) | copy-done | bytes 32792
  6.2 55.1 %sinkhorn.1 = (f32[128,128]{1,0:T(8,128)S(1)}, f32[64,128]{1,0:T(8,128)S(1)}) custom-call(s32[1,1]{1,0:T(1,128)S(6)} %copy.12.count, s32[1,64]{1,0:T(1,128)S(1)} %bitcast.12, s32[1,64]{1,0:T(1,128)S(1)} %bitcast.13, s32[3,16384]{1,0:T(4,128)S(1)} %copy-done, s32[3,8192]{1,0:T(4,128)S(1)} %copy-done.1, s32[8,16,128]{2,1,0:T(8,128)S(1)} %bitcast.7, ...), custom_call_target="tpu_custom_call" | custom-call | tf_op jit(solution)/shard_map/sinkhorn/pallas_call | solution.py:273
  61.2 0.6 %copy.13 = f32[16384]{0:T(1024)} copy(f32[16384]{0:T(1024)S(1)} %bitcast.8) | data formatting | bytes 131072
  61.9 0.6 copy.14
Async XLA Ops:
  1.3 0.7 %copy-start.5 = (s32[1,1,64]{2,1,0:T(1,128)S(1)}, s32[1,1,64]{2,1,0:T(1,128)}, u32[]{:S(2)}) copy-start(s32[1,1,64]{2,1,0:T(1,128)} %param.13) | copy-start | bytes 772
  1.3 0.7 %copy-start.6 = (s32[1,1,64]{2,1,0:T(1,128)S(1)}, s32[1,1,64]{2,1,0:T(1,128)}, u32[]{:S(2)}) copy-start(s32[1,1,64]{2,1,0:T(1,128)} %param.14) | copy-start | bytes 772
  2.0 0.9 %copy-start = (s32[3,16384]{1,0:T(4,128)S(1)}, s32[3,16384]{1,0:T(4,128)}, u32[]{:S(2)}) copy-start(s32[3,16384]{1,0:T(4,128)} %src_xyz_in.1) | copy-start | bytes 589828
  2.9 0.9 %copy-start.1 = (s32[3,8192]{1,0:T(4,128)S(1)}, s32[3,8192]{1,0:T(4,128)}, u32[]{:S(2)}) copy-start(s32[3,8192]{1,0:T(4,128)} %tgt_xyz_in.1) | copy-start | bytes 294916
  3.8 0.8 %copy-start.2 = (s32[16384]{0:T(1024)S(1)}, s32[16384]{0:T(1024)}, u32[]{:S(2)}) copy-start(s32[16384]{0:T(1024)} %param.10) | copy-start | bytes 196612
  4.6 0.8 %copy-start.3 = (s32[8192]{0:T(1024)S(1)}, s32[8192]{0:T(1024)}, u32[]{:S(2)}) copy-start(s32[8192]{0:T(1024)} %param.11) | copy-start | bytes 98308
  5.4 0.8 %copy-start.4 = (f32[8192]{0:T(1024)S(1)}, f32[8192]{0:T(1024)}, u32[]{:S(2)}) copy-start(f32[8192]{0:T(1024)} %param.12) | copy-start | bytes 98308
where the time goes:
time: 62.9 us; the launch traced here: 62.5 us
  Pallas kernels  55.1 us (88%)
  local copies, waits for them, and re-layouts  6.11 us (10%)
  between operations  1.31 us (2%)
    pallas_call x1, Pallas kernels, on_device(): pl.pallas_call(functools.partial(kernel, n_row, n_col), out_shape=(jax.Sh...  55.1 us
    unnamed x16, local copies, waits for them, and re-layouts  6.11 us

commit v1 on v0

--- a/solution.py
+++ b/solution.py
@@ -55,8 +55,8 @@
 def kernel(
     n_row, n_col,
     count, kept_src, kept_tgt, src_xyz_in, tgt_xyz_in, src_mass_in, tgt_mass_in, start_in,
-    src_out, tgt_out,
-    src_ids, tgt_ids, src_xyz, tgt_xyz, src_mass, tgt_mass, start, load_sems,
+    out,
+    live_count, src_ids, tgt_ids, src_xyz, tgt_xyz, src_mass, tgt_mass, start, load_sems,
     idx_rows, idx, idx_sem, place_s, place_t,
     a_src, b_src, a_tgt, b_tgt, sq_src, sq_tgt, log_src, log_tgt,
     hat_src, hat_tgt, peak, total, runs, send_src, got_src, got_tgt,
@@ -71,7 +71,7 @@
         for k, (src, dst) in enumerate((
             (kept_src, src_ids), (kept_tgt, tgt_ids), (src_mass_in, src_mass),
             (tgt_mass_in, tgt_mass), (src_xyz_in, src_xyz), (tgt_xyz_in, tgt_xyz),
-            (start_in, start),
+            (start_in, start), (count, live_count),
         ))
     ]
     for load in loads:
@@ -84,9 +84,9 @@
                 barrier, inc=1, device_id={axis: lax.rem(me + off, n)}, device_id_type=MESH
             )
 
-    for load in loads[:2]:
+    for load in loads[:2] + loads[7:]:
         load.wait()
-    live = lax.broadcasted_iota(jnp.int32, (1, slots), 1) < count[0, 0]
+    live = lax.broadcasted_iota(jnp.int32, (1, slots), 1) < live_count[...]
     idx_rows[...] = jnp.zeros_like(idx_rows)
     for k, (ids, others, place, tiles) in enumerate((
         (src_ids, tgt_ids, place_s, a_src.shape[0]), (tgt_ids, src_ids, place_t, a_tgt.shape[0]),
@@ -136,7 +136,7 @@
 
         lax.fori_loop(0, a_ref.shape[0] // UNROLL, step, 0)
 
-    for load in loads[4:]:
+    for load in loads[4:7]:
         load.wait()
     set_up(src_xyz, a_src, b_src, sq_src)
     set_up(tgt_xyz, a_tgt, b_tgt, sq_tgt)
@@ -146,38 +146,57 @@
 
     def partials(load_hat, a_ref, b_ref, in_row, out_row, place):
         def step(block, carry):
-            for u in range(SLOT_UNROLL):
-                p = block * SLOT_UNROLL + u
-                i_in, i_out = idx[in_row, p], idx[out_row, p]
-                hat = jnp.broadcast_to(load_hat(i_in), (8, LANES))
-                high = hat.astype(jnp.bfloat16).astype(jnp.float32)
-                rest = hat - high
-                mid = rest.astype(jnp.bfloat16).astype(jnp.float32)
-                a = jnp.where(
-                    sublane == 3, high,
-                    jnp.where(sublane == 4, mid, jnp.where(sublane == 5, rest - mid, a_ref[i_in])),
-                ).astype(jnp.bfloat16)
+            for u in range(0, SLOT_UNROLL, 2):
+                lefts, rights = [], []
+                for v in range(2):
+                    p = block * SLOT_UNROLL + u + v
+                    i_in, i_out = idx[in_row, p], idx[out_row, p]
+                    hat = jnp.broadcast_to(load_hat(i_in), (8, LANES))
+                    high = hat.astype(jnp.bfloat16).astype(jnp.float32)
+                    rest = hat - high
+                    mid = rest.astype(jnp.bfloat16).astype(jnp.float32)
+                    low = rest - mid
+                    lefts.append(jnp.where(
+                        sublane == 3, high,
+                        jnp.where(sublane == 4, mid, jnp.where(sublane == 5, low, a_ref[i_in])),
+                    ))
+                    zero = jnp.zeros((8, LANES), jnp.float32)
+                    pair = [b_ref[i_out], zero] if v == 0 else [zero, b_ref[i_out]]
+                    rights.append(jnp.concatenate(pair, axis=1))
                 scores = lax.dot_general(
-                    a, b_ref[i_out].astype(jnp.bfloat16), (((0,), (0,)), ((), ())),
-                    preferred_element_type=jnp.float32,
+                    jnp.concatenate(lefts, axis=0).astype(jnp.bfloat16),
+                    jnp.concatenate(rights, axis=0).astype(jnp.bfloat16),
+                    (((0,), (0,)), ((), ())), preferred_element_type=jnp.float32,
                 )
-                top = jnp.max(scores, axis=0, keepdims=True)
-                peak[pl.ds(p, 1), :] = top
-                total[pl.ds(p, 1), :] = jnp.sum(
-                    jnp.exp2((scores - top) * EXP2), axis=0, keepdims=True
-                )
+                for v in range(2):
+                    p = block * SLOT_UNROLL + u + v
+                    part = scores[:, v * LANES : (v + 1) * LANES]
+                    top = jnp.max(part, axis=0, keepdims=True)
+                    peak[pl.ds(p, 1), :] = top
+                    total[pl.ds(p, 1), :] = jnp.sum(
+                        jnp.exp2((part - top) * EXP2), axis=0, keepdims=True
+                    )
             return carry
 
         lax.fori_loop(0, slots // SLOT_UNROLL, step, 0)
         where_in = place[...]
-        lse = jnp.where(where_in >= 0, peak[...] * COST + jnp.log(total[...]), NEG)
+        top, summed = peak[...], total[...]
         reach = 1
         while reach < slots:
-            before = pltpu.roll(lse, reach, axis=0)
-            both = jnp.maximum(lse, before) + jnp.log(1.0 + jnp.exp(-jnp.abs(lse - before)))
-            lse = jnp.where(where_in >= reach, both, lse)
+            top_before = pltpu.roll(top, reach, axis=0)
+            sum_before = pltpu.roll(summed, reach, axis=0)
+            both = jnp.maximum(top, top_before)
+            low = jnp.exp2((jnp.minimum(top, top_before) - both) * EXP2)
+            here = top >= top_before
+            both_sum = jnp.where(here, summed, sum_before) + low * jnp.where(
+                here, sum_before, summed
+            )
+            joined = where_in >= reach
+            top, summed = jnp.where(joined, both, top), jnp.where(joined, both_sum, summed)
             reach *= 2
-        runs[pl.ds(0, slots), :] = lse
+        runs[pl.ds(0, slots), :] = jnp.where(
+            where_in >= 0, top * COST + jnp.log(summed), NEG
+        )
 
     def send(axis, me, n, off, src, dst, sems):
         copy = pltpu.make_async_remote_copy(
@@ -255,9 +274,9 @@
     log_src[...] = jnp.log(src_mass[col].astype(jnp.float32)) - jnp.log(src_all)
     log_tgt[...] = jnp.log(tgt_mass[...].astype(jnp.float32)) - jnp.log(tgt_all)
     lax.fori_loop(0, ITERS, iterate, 0)
-    src_hat = hat_src[ITERS - 1].reshape(src_out.shape)
-    src_out[...] = (src_hat + sq_src[...]) * COST
-    tgt_out[...] = (hat_tgt[ITERS] + sq_tgt[...]) * COST
+    src_tiles = sq_src.shape[0]
+    out[0:src_tiles, :] = (hat_src[ITERS - 1].reshape(sq_src.shape) + sq_src[...]) * COST
+    out[src_tiles:, :] = (hat_tgt[ITERS] + sq_tgt[...]) * COST
 
 
 def on_device(
@@ -269,16 +288,13 @@
     src_split = (n_col, src_tiles // n_col, LANES)
     src_block, tgt_block = (src_tiles, LANES), (tgt_tiles, LANES)
     f32, i32 = jnp.float32, jnp.int32
-    vmem = pl.BlockSpec(memory_space=pltpu.VMEM)
-    src_out, tgt_out = pl.pallas_call(
+    out = pl.pallas_call(
         functools.partial(kernel, n_row, n_col),
-        out_shape=(
-            jax.ShapeDtypeStruct(src_block, f32),
-            jax.ShapeDtypeStruct(tgt_block, f32),
-        ),
-        in_specs=[pl.BlockSpec(memory_space=pltpu.SMEM)] + [pl.BlockSpec(memory_space=pl.ANY)] * 7,
-        out_specs=(vmem, vmem),
+        out_shape=jax.ShapeDtypeStruct((src_tiles + tgt_tiles, LANES), f32),
+        in_specs=[pl.BlockSpec(memory_space=pl.ANY)] * 8,
+        out_specs=pl.BlockSpec(memory_space=pltpu.VMEM),
         scratch_shapes=[
+            pltpu.VMEM((1, 1), i32),
             pltpu.VMEM((1, slots), i32),
             pltpu.VMEM((1, slots), i32),
             pltpu.VMEM(src_coords.shape, i32),
@@ -286,7 +302,7 @@
             pltpu.VMEM(src_split, i32),
             pltpu.VMEM(tgt_block, i32),
             pltpu.VMEM(tgt_block, f32),
-            pltpu.SemaphoreType.DMA((7,)),
+            pltpu.SemaphoreType.DMA((8,)),
             pltpu.VMEM((8, LANES), i32),
             pltpu.SMEM((8, LANES), i32),
             pltpu.SemaphoreType.DMA,
@@ -315,7 +331,7 @@
             pltpu.SemaphoreType.DMA((ITERS, 2, n_row - 1)),
         ],
         compiler_params=pltpu.CompilerParams(
-            collective_id=0, has_side_effects=True, vmem_limit_bytes=48 * 1024 * 1024
+            collective_id=0, has_side_effects=True, vmem_limit_bytes=56 * 1024 * 1024
         ),
         name="sinkhorn",
     )(
@@ -323,7 +339,7 @@
         src_coords, tgt_coords,
         src_mass.reshape(src_split), tgt_mass.reshape(tgt_block), tgt_start.reshape(tgt_block),
     )
-    return src_out.reshape(-1), tgt_out.reshape(-1)
+    return out[:src_tiles].reshape(-1), out[src_tiles:].reshape(-1)
 
 
 def solution(mesh):

time: 62.9 us -> 59 us (0.938)
  local copies, waits for them, and re-layouts: 6.11 us -> 2.85 us
    unnamed x16 -> x0, local copies, waits for them, and re-layouts: 6.11 us -> none
    reshape x0 -> x2, local copies, waits for them, and re-layouts: none -> 2.85 us  [on_device(): return (out[:src_tiles].reshape(-1), out[src_tiles:].reshape(-1))]
where the time goes in v1:
time: 59 us; the launch traced here: 58.8 us
  Pallas kernels  54.6 us (93%)
  local copies, waits for them, and re-layouts  2.85 us (5%)
  between operations  1.29 us (2%)
    pallas_call x1, Pallas kernels, on_device(): pl.pallas_call(functools.partial(kernel, n_row, n_col), out_shape=jax.Sha...  54.6 us
    reshape x2, local copies, waits for them, and re-layouts, on_device(): return (out[:src_tiles].reshape(-1), out[src_tiles:].reshape(-1))  2.85 us

profile of v1, /device:TPU:0, one launch (start us, length us, event | category | flops | bytes accessed | tf_op | source)
XLA Modules:
  0.0 58.8 jit_solution(18315786836265678262)
XLA Ops:
  1.3 54.6 %sinkhorn.1 = f32[192,128]{1,0:T(8,128)} custom-call(s32[1,1]{1,0:T(1,128)S(6)} %copy.10.count, s32[1,64]{1,0:T(1,128)} %bitcast.12, s32[1,64]{1,0:T(1,128)} %bitcast.13, s32[3,16384]{1,0:T(4,128)} %src_xyz_in.1, s32[3,8192]{1,0:T(4,128)} %tgt_xyz_in.1, s32[8,16,128]{2,1,0:T(8,128)} %bitcast.9, s32[64,128]{1,0:T(8,128)} %bitcast.10, f32[64,128]{1,0:T(8,128)} %bitcast.11), custom_call_target="tpu_custom_call" | custom-call | tf_op jit(solution)/shard_map/sinkhorn/pallas_call | solution.py:291
  55.9 1.4 %slice_bitcast_fusion.1 = f32[8192]{0:T(1024)} fusion(f32[192,128]{1,0:T(8,128)} %sinkhorn.1), kind=kLoop, calls=%fused_computation.1 | loop fusion | bytes 65536 | tf_op jit(solution)/shard_map/reshape | solution.py:342
  57.3 1.5 %slice_bitcast_fusion = f32[16384]{0:T(1024)} fusion(f32[192,128]{1,0:T(8,128)} %sinkhorn.1), kind=kLoop, calls=%fused_computation | loop fusion | bytes 131072 | tf_op jit(solution)/shard_map/reshape | solution.py:342
